TPU v7x, 32 devices: a whole 2x2x4 slice. The times are simulated.
32 devices in a mesh: req: 8 (over z, y), head: 4 (over x, core).
Axes of the slice: x: 2, y: 2, z: 4, core: 2. Of those that a mesh axis runs over, the one named last changes fastest.
Arguments:
- queries: bfloat16 [2048, 8192], P('req', 'head'), may hold values from -8 to 8
- new_keys: bfloat16 [2048, 1024], P('req'), may hold values from -5 to 5
- new_values: bfloat16 [2048, 1024], P('req'), may hold values from -24 to 24
- cache_keys: bfloat16 [16, 256, 1024], P('req'), may hold values from -4 to 4
- cache_values: bfloat16 [16, 256, 1024], P('req'), may hold values from -24 to 24
- request_slot: int32 [8], P('req'), may hold values from 0 to 1
- tenant_ids: int32 [2048], P('req'), may hold values from 0 to 127
- out_weight: bfloat16 [8192, 8192], P('req', 'head'), may hold values from -0.0625 to 0.0625
- adapter_down: bfloat16 [8192, 4096], P('head', 'req'), may hold values from -0.0625 to 0.0625
- adapter_up: bfloat16 [4096, 8192], P('req', 'head'), may hold values from -1 to 1
Outputs:
- mixed: bfloat16 [2048, 8192], P('req', 'head')
All inputs are finite; a program needn't handle non-finite values.
Results may differ from a plain program's by a relative error of at most 0.0064.
Values may be sent and summed in bfloat16 or wider, within the bound.
A program may use at most 128 MiB of HBM per device.

v0:
```python
import jax
import jax.numpy as jnp
from jax import lax
from jax.sharding import PartitionSpec as P

HEADS = 64
HD = 128
KVH = 8
RANK = 32


def pick_heads(block, shared_index):
    spread = block.reshape(block.shape[0], KVH, HD)
    return jnp.take(spread, shared_index, axis=1)


def select(tenants, count):
    return tenants[:, None] == jnp.arange(count, dtype=jnp.int32)[None, :]


def shrink(block, tenants, weights):
    count = weights.shape[1] // RANK
    product = jnp.dot(block, weights, preferred_element_type=jnp.float32)
    product = product.reshape(block.shape[0], count, RANK)
    chosen = select(tenants, count).astype(jnp.float32)
    return jnp.sum(product * chosen[:, :, None], axis=1)


def expand(shrunk, tenants, weights):
    count = weights.shape[0] // RANK
    chosen = select(tenants, count).astype(jnp.bfloat16)
    spread = (chosen[:, :, None] * shrunk[:, None, :]).reshape(shrunk.shape[0], count * RANK)
    return jnp.dot(spread, weights, preferred_element_type=jnp.float32)


def attention(queries, new_keys, new_values, cache_keys, cache_values, request_slot):
    row_count = queries.shape[0]
    local_heads = queries.shape[1] // HD
    group = HEADS // KVH
    shared_index = (
        lax.axis_index("head") * local_heads + jnp.arange(local_heads, dtype=jnp.int32)
    ) // group
    slot_index = request_slot[0]
    keys_old = pick_heads(
        lax.dynamic_index_in_dim(cache_keys, slot_index, 0, keepdims=False), shared_index
    )
    values_old = pick_heads(
        lax.dynamic_index_in_dim(cache_values, slot_index, 0, keepdims=False), shared_index
    )
    keys_new = pick_heads(new_keys, shared_index)
    values_new = pick_heads(new_values, shared_index)
    split_queries = queries.reshape(row_count, local_heads, HD)
    scale = HD ** (-0.5)
    scores_old = (
        jnp.einsum("qhd,khd->hqk", split_queries, keys_old, preferred_element_type=jnp.float32)
        * scale
    )
    scores_new = (
        jnp.einsum("qhd,khd->hqk", split_queries, keys_new, preferred_element_type=jnp.float32)
        * scale
    )
    causal = (
        jnp.arange(row_count, dtype=jnp.int32)[:, None]
        >= jnp.arange(row_count, dtype=jnp.int32)[None, :]
    )
    scores_new = jnp.where(causal[None], scores_new, -1e30)
    highest = jnp.maximum(jnp.max(scores_old, axis=2), jnp.max(scores_new, axis=2))[:, :, None]
    weights_old = jnp.exp(scores_old - highest)
    weights_new = jnp.where(causal[None], jnp.exp(scores_new - highest), 0.0)
    total = jnp.sum(weights_old, axis=2, keepdims=True) + jnp.sum(
        weights_new, axis=2, keepdims=True
    )
    probs_old = (weights_old / total).astype(jnp.bfloat16)
    probs_new = (weights_new / total).astype(jnp.bfloat16)
    output = jnp.einsum("hqk,khd->qhd", probs_old, values_old, preferred_element_type=jnp.float32)
    output = output + jnp.einsum(
        "hqk,khd->qhd", probs_new, values_new, preferred_element_type=jnp.float32
    )
    return output.reshape(row_count, local_heads * HD).astype(jnp.bfloat16)


def local(
    queries,
    new_keys,
    new_values,
    cache_keys,
    cache_values,
    request_slot,
    tenant_ids,
    out_weight,
    adapter_down,
    adapter_up,
):
    attended = attention(queries, new_keys, new_values, cache_keys, cache_values, request_slot)
    partial_value = shrink(
        attended, tenant_ids, lax.all_gather(adapter_down, "req", axis=1, tiled=True)
    )
    shrunk = lax.psum(partial_value, "head").astype(jnp.bfloat16)
    features = lax.all_gather(attended, "head", axis=1, tiled=True)
    base = jnp.dot(
        features,
        lax.all_gather(out_weight, "req", axis=0, tiled=True),
        preferred_element_type=jnp.float32,
    )
    summed = expand(shrunk, tenant_ids, lax.all_gather(adapter_up, "req", axis=0, tiled=True))
    delta = lax.optimization_barrier(summed.astype(jnp.bfloat16)).astype(jnp.float32)
    return (base + delta).astype(jnp.bfloat16)


def solution(mesh):
    placed = (
        P("req", "head"),
        P("req", None),
        P("req", None),
        P("req", None, None),
        P("req", None, None),
        P("req"),
        P("req"),
        P("req", "head"),
        P("head", "req"),
        P("req", "head"),
    )
    return jax.shard_map(
        local, mesh=mesh, in_specs=placed, out_specs=P("req", "head"), check_vma=False
    )
```

profile of v0, /device:TPU:0, one launch (start us, length us, event | category | flops | bytes accessed | tf_op | source)
XLA Modules:
  0.0 1166.4 jit_solution(5055061279197391969)
XLA Ops:
  6.5 0.0 copy-start
  6.5 0.0 copy-start.7
  6.5 0.0 all-gather.9.cloned.1.call-start
  6.5 4.1 copy.40
  10.6 0.0 copy-start.6
  10.6 0.0 all-gather.9.cloned.1.call-update
  10.7 0.0 all-gather.11.cloned.1.call-start
  10.7 0.7 all-gather.11.cloned.1.call-update
  11.4 0.0 all-gather.5.cloned.1.call-start
  12.1 0.0 copy-done.7
  12.1 1.9 constant_dynamic-slice_fusion
  14.1 0.2 copy.50
  14.3 0.3 copy.29
  14.5 0.0 copy-done.6
  14.6 0.2 copy.31
  14.8 0.3 copy.32
  15.1 0.7 gather_fusion.1
  15.8 1.7 gather_fusion.2
  17.5 1.2 copy.49
  18.7 0.3 copy.27
  19.0 1.6 gather_fusion
  20.7 1.3 copy.36
  22.0 0.3 copy.37
  22.3 1.7 gather_fusion.3
  24.0 0.0 copy-start.4
  24.0 0.0 copy-done
  24.0 0.8 bitcast_reduce_fusion
  24.8 0.5 copy-done.4
  25.3 0.9 fusion.3
  26.2 0.0 copy-start.2
  26.2 1.7 fusion.5
  28.0 0.0 copy-done.2
  28.0 0.0 copy-start.3
  28.0 1.4 fusion.7
  29.4 0.0 copy-done.3
  29.5 2.6 add_convert_fusion
  32.1 0.0 copy-start.8
  32.1 0.0 copy-start.5
  32.1 0.0 all-gather.5.cloned.1.call-update
  32.1 0.2 all-gather.7.cloned.1.call-start
  32.3 0.3 all-gather.7.cloned.1.call-update
  32.7 0.1 copy-done.8
  32.8 208.4 %all-gather.9.cloned.1.call-done = bf16[2048,4096]{0,1:T(8,128)(2,1)} async-done(((bf16[2048,512]{0,1:T(8,128)(2,1)}), bf16[2048,4096]{0,1:T(8,128)(2,1)}) %all-gather.9.cloned.1.call-update) | async-done | bytes 16777232 | tf_op jit(solution)/shard_map/all_gather | solution.py:96
  241.1 0.0 copy-done.5
  241.1 26.1 %multiply_reduce_fusion = f32[256,32]{0,1:T(8,128)S(1)} fusion(f32[256,128]{0,1:T(8,128)S(1)} %get-tuple-element.9, bf16[256,2048,1]{0,1,2:T(8,128)(2,1)S(1)} %bitcast.83, bf16[128,32,2048]{2,1,0:T(8,128)(2,1)} %bitcast.84), kind=kOutput, calls=%fused_computation.10 | convolution fusion | flops 4297056256 | bytes 17989632 | tf_op jit(solution)/shard_map/dot_general | solution.py:23
  267.2 11.5 psum.7
  278.7 0.1 broadcast_multiply_fusion
  278.8 190.3 %all-gather.11.cloned.1.call-done = bf16[4096,2048]{1,0:T(8,128)(2,1)} async-done(((bf16[512,2048]{1,0:T(8,128)(2,1)}), bf16[4096,2048]{1,0:T(8,128)(2,1)}) %all-gather.11.cloned.1.call-update) | async-done | bytes 16777232 | tf_op jit(solution)/shard_map/all_gather | solution.py:105
  469.1 9.3 convolution_convert_fusion
  478.4 24.9 %all-gather.5.cloned.1.call-done = bf16[256,8192]{0,1:T(8,128)(2,1)} async-done(((bf16[256,2048]{0,1:T(8,128)(2,1)}), bf16[256,8192]{0,1:T(8,128)(2,1)}) %all-gather.5.cloned.1.call-update) | async-done | bytes 4194320 | tf_op jit(solution)/shard_map/all_gather | solution.py:99
  503.3 639.2 %all-gather.7.cloned.1.call-done = bf16[8192,2048]{1,0:T(8,128)(2,1)} async-done(((bf16[1024,2048]{1,0:T(8,128)(2,1)}), bf16[8192,2048]{1,0:T(8,128)(2,1)}) %all-gather.7.cloned.1.call-update) | async-done | bytes 33554448 | tf_op jit(solution)/shard_map/all_gather | solution.py:102
  1142.5 0.0 copy-start.1
  1142.5 17.3 %fusion.6 = bf16[256,2048]{1,0:T(8,128)(2,1)} fusion(bf16[256,8192]{0,1:T(8,128)(2,1)} %all-gather.5.cloned.1.call-done, bf16[8192,2048]{1,0:T(8,128)(2,1)} %all-gather.7.cloned.1.call-done, bf16[256,2048]{1,0:T(8,128)(2,1)} %convolution_convert_fusion), kind=kOutput, calls=%fused_computation.18 | convolution fusion | flops 8591507456 | bytes 39845888 | tf_op jit(solution)/shard_map/dot_general | solution.py:100
  1159.8 0.0 copy-done.1
  (7 shorter events, 0.1 us)
Async XLA Ops:
  6.5 17.5 %copy-start = (bf16[256,2048]{1,0:T(8,128)(2,1)S(1)}, bf16[256,2048]{1,0:T(8,128)(2,1)}, u32[]{:S(2)}) copy-start(bf16[256,2048]{1,0:T(8,128)(2,1)} %param.12) | copy-start | bytes 3145732
  6.5 5.6 copy-start.7
  6.5 234.6 %all-gather.9.cloned.1.call-start = ((), (), s32[]{:S(2)}) async-start(), calls=%async_computation.2 | async-start | bytes 18874368 | tf_op jit(solution)/shard_map/all_gather | solution.py:96
  10.6 3.9 copy-start.6
  10.7 458.4 %all-gather.11.cloned.1.call-start = ((), (), s32[]{:S(2)}) async-start(), calls=%async_computation.3 | async-start | bytes 18874368 | tf_op jit(solution)/shard_map/all_gather | solution.py:105
  11.4 491.9 %all-gather.5.cloned.1.call-start = ((), (), s32[]{:S(2)}) async-start(), calls=%async_computation | async-start | bytes 5242880 | tf_op jit(solution)/shard_map/all_gather | solution.py:99
  24.0 1.3 copy-start.4
  26.2 1.7 copy-start.2
  28.0 1.5 copy-start.3
  32.1 0.7 copy-start.8
  32.1 209.1 %copy-start.5 = (bf16[16,128,256]{2,1,0:T(8,128)(2,1)S(1)}, bf16[16,128,256]{2,1,0:T(8,128)(2,1)}, u32[]{:S(2)}) copy-start(bf16[16,128,256]{2,1,0:T(8,128)(2,1)} %add_convert_fusion) | copy-start | bytes 3145732
  32.1 1110.4 %all-gather.7.cloned.1.call-start = ((), (), s32[]{:S(2)}) async-start(), calls=%async_computation.1 | async-start | bytes 37748736 | tf_op jit(solution)/shard_map/all_gather | solution.py:102
  1142.5 17.3 %copy-start.1 = (bf16[256,2048]{1,0:T(8,128)(2,1)S(1)}, bf16[256,2048]{1,0:T(8,128)(2,1)}, u32[]{:S(2)}) copy-start(bf16[256,2048]{1,0:T(8,128)(2,1)} %param.12) | copy-start | bytes 3145732
Sparse Core Ops, SparseCore 0:
  10.8 230.2 all-gather.8
  243.3 225.7 all-gather.10
  470.6 32.6 all-gather.4
  504.7 637.7 all-gather.6
where the time goes:
time: 1170 us
  waiting for transfers between devices  1060 us (91%)
  matrix products  58.4 us (5%)
  local copies, waits for them, and re-layouts  16.4 us (1%)
  between operations  14 us (1%)
    all_gather x1, waiting for transfers between devices, local(): lax.all_gather(out_weight, 'req', axis=0, tiled=True)  639 us
    all_gather x1, waiting for transfers between devices, local(): lax.all_gather(adapter_down, 'req', axis=1, tiled=True)  208 us
    all_gather x1, waiting for transfers between devices, local(): lax.all_gather(adapter_up, 'req', axis=0, tiled=True)  190 us
    dot_general x1, matrix products, shrink(): product = jnp.dot(block, weights, preferred_element_type=jnp.float32)  26.1 us
    all_gather x1, waiting for transfers between devices, local(): features = lax.all_gather(attended, 'head', axis=1, tiled=True)  24.9 us
  transfers between devices with their start and end apart: 4, of which 4 were waited for; matrix products, arithmetic and copies ran while one was open for 5% of the time, Pallas kernels for 0%

commit v1 on v0

--- a/solution.py
+++ b/solution.py
@@ -18,19 +18,53 @@
     return tenants[:, None] == jnp.arange(count, dtype=jnp.int32)[None, :]
 
 
-def shrink(block, tenants, weights):
+def reshard_down(weights):
+    count = lax.axis_size("req")
+    heads = lax.axis_size("head")
+    fold = count // heads
+    rows = weights.shape[0] // fold
+    mine = lax.axis_index("req") % fold
+    spread = weights.reshape(fold, rows, weights.shape[1])
+    received = []
+    for shift in range(fold):
+        piece = lax.dynamic_index_in_dim(spread, (mine + shift) % fold, 0, keepdims=False)
+        pairs = []
+        for source in range(count):
+            outer, inner = source // fold, source % fold
+            for head in range(heads):
+                target = head * fold + (inner + shift) % fold
+                pairs.append((source * heads + head, target * heads + outer))
+        received.append(lax.ppermute(piece, ("req", "head"), pairs))
+    stacked = jnp.stack(received, axis=0)
+    order = (mine - jnp.arange(fold, dtype=jnp.int32)) % fold
+    stacked = jnp.take(stacked, order, axis=0)
+    return jnp.transpose(stacked, (1, 0, 2)).reshape(rows, fold * weights.shape[1])
+
+
+def gather_features(attended):
+    count = lax.axis_size("req")
+    heads = lax.axis_size("head")
+    quarter = lax.all_to_all(attended, "head", 0, 1, tiled=True)
+    part = lax.all_to_all(quarter, "req", 1, 0, tiled=True)
+    full = lax.all_gather(part, "head", axis=0, tiled=False)
+    rows = attended.shape[0] // heads
+    full = full.reshape(heads, count, rows, part.shape[1])
+    return jnp.transpose(full, (1, 0, 2, 3)).reshape(count * attended.shape[0], part.shape[1])
+
+
+def shrink(block, tenants, weights, first):
     count = weights.shape[1] // RANK
     product = jnp.dot(block, weights, preferred_element_type=jnp.float32)
     product = product.reshape(block.shape[0], count, RANK)
-    chosen = select(tenants, count).astype(jnp.float32)
-    return jnp.sum(product * chosen[:, :, None], axis=1)
+    chosen = tenants[:, None] == first + jnp.arange(count, dtype=jnp.int32)[None, :]
+    return jnp.sum(jnp.where(chosen[:, :, None], product, 0.0), axis=1)
 
 
-def expand(shrunk, tenants, weights):
-    count = weights.shape[0] // RANK
-    chosen = select(tenants, count).astype(jnp.bfloat16)
-    spread = (chosen[:, :, None] * shrunk[:, None, :]).reshape(shrunk.shape[0], count * RANK)
-    return jnp.dot(spread, weights, preferred_element_type=jnp.float32)
+def spread_tenants(shrunk, tenants, count, first):
+    chosen = tenants[:, None] == first + jnp.arange(count, dtype=jnp.int32)[None, :]
+    return jnp.where(chosen[:, :, None], shrunk[:, None, :], 0).reshape(
+        shrunk.shape[0], count * RANK
+    )
 
 
 def attention(queries, new_keys, new_values, cache_keys, cache_values, request_slot):
@@ -91,20 +125,20 @@
     adapter_down,
     adapter_up,
 ):
+    down = reshard_down(adapter_down)
+    tenants = lax.all_gather(tenant_ids, "req", axis=0, tiled=True)
     attended = attention(queries, new_keys, new_values, cache_keys, cache_values, request_slot)
-    partial_value = shrink(
-        attended, tenant_ids, lax.all_gather(adapter_down, "req", axis=1, tiled=True)
+    block = gather_features(attended)
+    down_count = down.shape[1] // RANK
+    up_count = adapter_up.shape[0] // RANK
+    part = shrink(block, tenants, down, lax.axis_index("head") * down_count)
+    shrunk = lax.psum(part, ("req", "head")).astype(jnp.bfloat16)
+    spread = spread_tenants(shrunk, tenants, up_count, lax.axis_index("req") * up_count)
+    mixed = jnp.dot(block, out_weight, preferred_element_type=jnp.float32)
+    mixed = mixed + jnp.dot(spread, adapter_up, preferred_element_type=jnp.float32)
+    return lax.psum_scatter(
+        mixed.astype(jnp.bfloat16), "req", scatter_dimension=0, tiled=True
     )
-    shrunk = lax.psum(partial_value, "head").astype(jnp.bfloat16)
-    features = lax.all_gather(attended, "head", axis=1, tiled=True)
-    base = jnp.dot(
-        features,
-        lax.all_gather(out_weight, "req", axis=0, tiled=True),
-        preferred_element_type=jnp.float32,
-    )
-    summed = expand(shrunk, tenant_ids, lax.all_gather(adapter_up, "req", axis=0, tiled=True))
-    delta = lax.optimization_barrier(summed.astype(jnp.bfloat16)).astype(jnp.float32)
-    return (base + delta).astype(jnp.bfloat16)
 
 
 def solution(mesh):

time: 1170 us -> 445 us (0.38)
  waiting for transfers between devices: 1060 us -> 149 us
  blocking collectives: 11.5 us -> 184 us
  local copies, waits for them, and re-layouts: 16.4 us -> 39.4 us
  matrix products: 58.4 us -> 37.8 us
    all_gather x4 -> x1, waiting for transfers between devices: 1060 us -> 0.01 us  [gather_features(): full = lax.all_gather(part, 'head', axis=0, tiled=False)]
    reduce_scatter x0 -> x1, waiting for transfers between devices: none -> 149 us  [local(): lax.psum_scatter(mixed.astype(jnp.bfloat16), 'req', scatter_dimension=0,...]
    psum x1, blocking collectives: 11.5 us -> 85.1 us  [local(): shrunk = lax.psum(part, ('req', 'head')).astype(jnp.bfloat16)]
    all_to_all x0 -> x2, blocking collectives: none -> 50.6 us  [the longest x1 31.9 us: gather_features(): part = lax.all_to_all(quarter, 'req', 1, 0, tiled=True)]
    all_gather x0 -> x1, blocking collectives: none -> 48.2 us  [local(): tenants = lax.all_gather(tenant_ids, 'req', axis=0, tiled=True)]
    dot_general x1, matrix products: 26.1 us -> 4.81 us  [shrink(): product = jnp.dot(block, weights, preferred_element_type=jnp.float32)]
  transfers between devices with their start and end apart: 4 -> 4, of which waited for: 4 -> 1; matrix products, arithmetic and copies ran while one was open for 5% -> 4% of each run, Pallas kernels for 0% -> 0%
where the time goes in v1:
time: 445 us; the launch traced here: 444 us
  blocking collectives  184 us (41%)
  waiting for transfers between devices  149 us (33%)
  local copies, waits for them, and re-layouts  39.4 us (9%)
  matrix products  37.8 us (8%)
  between operations  14.5 us (3%)
  starting transfers between devices  10.9 us (2%)
  other arithmetic  8.48 us (2%)
    reduce_scatter x1, waiting for transfers between devices, local(): lax.psum_scatter(mixed.astype(jnp.bfloat16), 'req', scatter_dimension=0,...  149 us
    psum x1, blocking collectives, local(): shrunk = lax.psum(part, ('req', 'head')).astype(jnp.bfloat16)  85.1 us
    all_gather x1, blocking collectives, local(): tenants = lax.all_gather(tenant_ids, 'req', axis=0, tiled=True)  48.2 us
    all_to_all x1, blocking collectives, gather_features(): part = lax.all_to_all(quarter, 'req', 1, 0, tiled=True)  31.9 us
    all_to_all x1, blocking collectives, gather_features(): quarter = lax.all_to_all(attended, 'head', 0, 1, tiled=True)  18.7 us
    dot_general x1, matrix products, local(): mixed = jnp.dot(block, out_weight, preferred_element_type=jnp.float32)  15.2 us
    ppermute x2, starting transfers between devices, reshard_down(): received.append(lax.ppermute(piece, ('req', 'head'), pairs))  10.9 us
    dot_general x1, matrix products, local(): jnp.dot(spread, adapter_up, preferred_element_type=jnp.float32)  10.3 us
  transfers between devices with their start and end apart: 4, of which 1 were waited for; matrix products, arithmetic and copies ran while one was open for 4% of the time, Pallas kernels for 0%

profile of v1, /device:TPU:0, one launch (start us, length us, event | category | flops | bytes accessed | tf_op | source)
XLA Modules:
  0.0 443.9 jit_solution(15973137718963128262)
XLA Ops:
  6.5 0.0 copy-start
  6.5 0.0 all-gather.3.cloned.1.call-start
  7.4 1.2 copy.49
  8.7 0.3 copy.50
  8.9 2.0 copy.54
  11.0 1.3 copy.55
  12.3 1.7 gather_fusion.3
  14.0 1.7 gather_fusion.4
  15.7 1.3 constant_dynamic-slice_fusion
  16.9 1.0 copy.68
  17.9 1.3 copy.47
  19.3 1.7 gather_fusion.2
  20.9 1.0 copy.67
  21.9 1.3 copy.45
  23.2 1.7 gather_fusion.1
  24.9 0.0 copy-start.3
  24.9 0.0 copy-start.5
  24.9 2.5 bitcast_reduce_fusion
  27.4 0.0 copy-done.3
  27.4 0.0 copy-done.5
  27.4 0.9 fusion.1
  28.4 0.0 copy-start.6
  28.4 1.7 fusion.3
  30.1 0.0 copy-done.6
  30.1 0.0 copy-start.4
  30.1 1.4 fusion.4
  31.6 0.0 copy-done.4
  31.6 2.6 fusion.7
  34.2 1.9 copy.58
  36.1 1.3 convert_element_type.28
  37.4 18.7 %all_to_all.29 = bf16[4,64,2048]{2,1,0:T(8,128)(2,1)S(1)} all-to-all(bf16[4,64,2048]{2,1,0:T(8,128)(2,1)} %convert_element_type.28), channel_id=1, replica_groups=mesh['req'=8,'head'=4] {'head'}, dimensions={0} | all-to-all | bytes 2097152 | tf_op jit(solution)/shard_map/all_to_all | solution.py:47
  56.1 0.8 copy.59
  56.9 1.1 all_to_all.24
  58.0 1.8 copy.60
  59.8 0.0 copy-start.7
  59.8 31.9 %all_to_all.30 = bf16[64,8,1024]{2,0,1:T(8,128)(2,1)} all-to-all(bf16[64,8,1024]{2,0,1:T(8,128)(2,1)S(1)} %copy.60), channel_id=1, replica_groups=mesh['req'=8,'head'=4] {'req'}, dimensions={1} | all-to-all | bytes 2097152 | tf_op jit(solution)/shard_map/all_to_all | solution.py:48
  91.7 0.0 all-gather.3.cloned.1.call-update
  91.7 0.0 reduce-scatter.2.cloned.1.call-start
  91.8 2.7 dynamic-slice_bitcast_fusion.1
  94.5 9.5 %collective-permute-start = (bf16[1024,512]{1,0:T(8,128)(2,1)}, bf16[1024,512]{1,0:T(8,128)(2,1)}, u32[]{:S(2)}, u32[]{:S(2)}) collective-permute-start(bf16[1024,512]{1,0:T(8,128)(2,1)} %get-tuple-element.8), channel_id=1, source_target_pairs={{0,0},{1,8},{2,16},{3,24},{4,4},{5,12},{6,20},{7,28},{8,1},{9,9},{... | collective-permute-start | bytes 3145736 | tf_op jit(solution)/shard_map/ppermute | solution.py:37
  104.0 1.4 collective-permute-start.1
  105.5 0.0 copy-done.7
  105.5 48.2 %all-gather = s32[8,1,256]{2,1,0:T(1,128)S(1)} all-gather(s32[1,1,256]{2,1,0:T(1,128)S(1)} %bitcast.116), channel_id=1, replica_groups=mesh['req'=8,'head'=4] {'req'}, dimensions={0}, use_global_device_ids=true | all-gather | bytes 9216 | tf_op jit(solution)/shard_map/all_gather | solution.py:129
  153.7 0.1 broadcast_compare_fusion.1
  153.8 0.1 broadcast_compare_fusion
  153.9 0.0 collective-permute-done
  153.9 0.0 collective-permute-done.1
  153.9 3.1 pad_maximum_fusion
  157.0 3.6 gather_fusion
  160.6 3.2 select_bitcast_fusion
  163.8 4.0 copy.62
  167.7 0.0 all-gather.3.cloned.1.call-done
  167.8 2.8 copy.61
  170.5 0.0 copy-start.1
  170.5 1.9 copy-done.1
  172.5 0.0 copy-done.2
  172.5 4.8 %select_reduce_fusion = f32[2048,32]{0,1:T(8,128)S(1)} fusion(pred[2048,32]{0,1:T(8,128)(4,1)S(1)} %broadcast_compare_fusion, bf16[2048,1024,1]{1,0,2:T(8,128)(2,1)S(1)} %bitcast.103, bf16[32,32,1024]{2,1,0:T(8,128)(2,1)S(1)} %bitcast.108), kind=kOutput, calls=%fused_computation.6 | convolution fusion | flops 4299096064 | bytes 6619136 | tf_op jit(solution)/shard_map/dot_general | solution.py:57
  177.3 85.1 %all-reduce.1 = bf16[2048,32]{0,1:T(8,128)(2,1)S(1)} all-reduce(f32[2048,32]{0,1:T(8,128)S(1)} %select_reduce_fusion), channel_id=1, replica_groups=mesh['req'=8,'head'=4] {'req','head'}, use_global_device_ids=true, to_apply=%region_5.7 | all-reduce | flops 65536 | bytes 393216 | tf_op jit(solution)/shard_map/psum | solution.py:135
  262.4 0.2 broadcast_select_fusion
  262.6 15.2 %fusion.41 = f32[2048,2048]{1,0:T(8,128)} fusion(bf16[2048,1024]{1,0:T(8,128)(2,1)} %bitcast.104, bf16[1024,2048]{1,0:T(8,128)(2,1)} %param.19), kind=kOutput, calls=%fused_computation.84 | convolution fusion | flops 8589934592 | bytes 25165824 | tf_op jit(solution)/shard_map/dot_general | solution.py:137
  277.8 0.0 copy-done
  277.8 10.3 %add_convert_fusion = bf16[2048,2048]{1,0:T(8,128)(2,1)} fusion(f32[2048,2048]{1,0:T(8,128)} %fusion.41, bf16[2048,512]{0,1:T(8,128)(2,1)S(1)} %bitcast.109, bf16[512,2048]{1,0:T(8,128)(2,1)S(1)} %copy-done), kind=kOutput, calls=%fused_computation.5 | convolution fusion | flops 4303355904 | bytes 29360128 | tf_op jit(solution)/shard_map/dot_general | solution.py:138
  288.1 0.0 reduce-scatter.2.cloned.1.call-update
  288.1 148.9 %reduce-scatter.2.cloned.1.call-done = bf16[256,2048]{1,0:T(8,128)(2,1)} async-done(((bf16[2048,2048]{1,0:T(8,128)(2,1)}), bf16[256,2048]{1,0:T(8,128)(2,1)}) %reduce-scatter.2.cloned.1.call-update) | async-done | bytes 1048592 | tf_op jit(solution)/shard_map/reduce_scatter | solution.py:139
  (12 shorter events, 0.1 us)
Async XLA Ops:
  6.5 271.2 %copy-start = (bf16[512,2048]{1,0:T(8,128)(2,1)S(1)}, bf16[512,2048]{1,0:T(8,128)(2,1)}, u32[]{:S(2)}) copy-start(bf16[512,2048]{1,0:T(8,128)(2,1)} %param.21) | copy-start | bytes 6291460
  6.5 161.2 %all-gather.3.cloned.1.call-start = ((), (), s32[]{:S(2)}) async-start(), calls=%async_computation.3 | async-start | bytes 5242880 | tf_op jit(solution)/shard_map/all_gather | solution.py:49
  24.9 2.5 copy-start.3
  24.9 2.5 copy-start.5
  28.4 1.7 copy-start.6
  30.1 1.4 copy-start.4
  59.8 45.7 %copy-start.7 = (s32[256]{0:T(256)S(1)}, s32[256]{0:T(256)}, u32[]{:S(2)}) copy-start(s32[256]{0:T(256)} %param.18) | copy-start | bytes 3076
  91.7 345.3 %reduce-scatter.2.cloned.1.call-start = ((), (), s32[]{:S(2)}) async-start(), calls=%async_computation.4 | async-start | bytes 9437184 | tf_op jit(solution)/shard_map/reduce_scatter | solution.py:139
  94.5 59.4 %collective-permute-start = (bf16[1024,512]{1,0:T(8,128)(2,1)}, bf16[1024,512]{1,0:T(8,128)(2,1)}, u32[]{:S(2)}, u32[]{:S(2)}) collective-permute-start(bf16[1024,512]{1,0:T(8,128)(2,1)} %get-tuple-element.8), channel_id=1, source_target_pairs={{0,0},{1,8},{2,16},{3,24},{4,4},{5,12},{6,20},{7,28},{8,1},{9,9},{... | collective-permute-start | bytes 3145736 | tf_op jit(solution)/shard_map/ppermute | solution.py:37
  104.0 49.9 %collective-permute-start.1 = (bf16[1024,512]{1,0:T(8,128)(2,1)S(1)}, bf16[1024,512]{1,0:T(8,128)(2,1)}, u32[]{:S(2)}, u32[]{:S(2)}) collective-permute-start(bf16[1024,512]{1,0:T(8,128)(2,1)S(1)} %get-tuple-element.9), channel_id=1, source_target_pairs={{0,4},{1,12},{2,20},{3,28},{4,0},{5,8},{6,16},{7,24},{8,5},{9,13},... | collective-permute-start | bytes 3145736 | tf_op jit(solution)/shard_map/ppermute | solution.py:37
  167.7 4.7 %copy-start.2 = (bf16[1024,2,512]{0,2,1:T(8,128)(2,1)S(1)}, bf16[1024,2,512]{0,2,1:T(8,128)(2,1)}, u32[]{:S(2)}) copy-start(bf16[1024,2,512]{0,2,1:T(8,128)(2,1)} %copy.62) | copy-start | bytes 6291460
  170.5 1.9 copy-start.1
Sparse Core Ops, SparseCore 0:
  91.9 50.2 all-gather.2
  288.2 148.7 reduce-scatter.1

commit v2 on v1

--- a/solution.py
+++ b/solution.py
@@ -1,6 +1,10 @@
+import functools
+
 import jax
 import jax.numpy as jnp
 from jax import lax
+from jax.experimental import pallas as pl
+from jax.experimental.pallas import tpu as pltpu
 from jax.sharding import PartitionSpec as P
 
 HEADS = 64
@@ -41,15 +45,378 @@
     return jnp.transpose(stacked, (1, 0, 2)).reshape(rows, fold * weights.shape[1])
 
 
+def remote(src, dst, send_sem, recv_sem, **axis):
+    return pltpu.make_async_remote_copy(
+        src_ref=src,
+        dst_ref=dst,
+        send_sem=send_sem,
+        recv_sem=recv_sem,
+        device_id=axis,
+        device_id_type=pl.DeviceIdType.MESH,
+    )
+
+
+def greet(barrier, **axis):
+    pl.semaphore_signal(barrier, inc=1, device_id=axis, device_id_type=pl.DeviceIdType.MESH)
+
+
+def gather_kernel(count, heads, x_ref, out_ref, send_a, recv_a, local_sem, send_b, recv_b, send_c, recv_c):
+    fold = count // heads
+    rows = x_ref.shape[0]
+    share = rows // heads
+    width = out_ref.shape[1]
+    peers = heads // 2
+    r = lax.axis_index("req")
+    h = lax.axis_index("head")
+    owner = r // fold
+    twin = h + 1 - 2 * (h % 2)
+    barrier = pltpu.get_barrier_semaphore()
+    for source in range(count):
+        @pl.when(jnp.logical_or(r != source, h != owner))
+        def _():
+            greet(barrier, req=source, head=owner)
+    for step in range(1, heads):
+        greet(barrier, req=r, head=(h + step) % heads)
+
+    @pl.when(h == owner)
+    def _():
+        pl.semaphore_wait(barrier, count + heads - 2)
+
+    @pl.when(h != owner)
+    def _():
+        pl.semaphore_wait(barrier, count + heads - 1)
+
+    def place(source, quarter):
+        return out_ref.at[pl.ds(pl.multiple_of(source * rows + quarter * share, share), share), :]
+
+    def first(step):
+        target = (step + r) % count
+        inner, quarter = target % fold, target // fold
+        goal = h * fold + inner
+        src = x_ref.at[
+            pl.ds(pl.multiple_of(quarter * share, share), share),
+            pl.ds(pl.multiple_of(inner * width, width), width),
+        ]
+        far = jnp.logical_or(goal != r, quarter != h)
+        copy = remote(src, place(r, quarter), send_a.at[step], recv_a.at[r], req=goal, head=quarter)
+        near = pltpu.make_async_copy(src, place(r, quarter), local_sem)
+        return far, copy, near
+
+    for step in range(count):
+        far, copy, near = first(step)
+        pl.when(far)(copy.start)
+        pl.when(jnp.logical_not(far))(near.start)
+
+    def direct(source, kind):
+        head = twin if kind == 0 else (h + 2 * kind) % heads
+        spot = place(source, h)
+        return remote(spot, spot, send_b.at[kind, source], recv_b.at[kind, source], req=r, head=head)
+
+    def forward(source, kind):
+        spot = place(source, (h + heads - 2 * kind) % heads)
+        return remote(spot, spot, send_c.at[kind, source], recv_c.at[kind, source], req=r, head=twin)
+
+    def pass_on(source):
+        for kind in range(1, peers):
+            direct(source, kind).wait_recv()
+            forward(source, kind).start()
+
+    for step in range(count):
+        source = (r + count - step) % count
+        spot = place(source, h)
+        here = jnp.logical_and(source == r, h == owner)
+
+        @pl.when(here)
+        def _():
+            pltpu.make_async_copy(spot, spot, local_sem).wait()
+
+        @pl.when(jnp.logical_not(here))
+        def _():
+            remote(spot, spot, send_a.at[0], recv_a.at[source], req=r, head=twin).wait_recv()
+
+        for kind in [*range(1, peers), 0]:
+            direct(source, kind).start()
+        if step:
+            pass_on((source + 1) % count)
+    pass_on((r + 1) % count)
+    for step in range(count):
+        far, copy, near = first(step)
+        pl.when(far)(copy.wait_send)
+    for source in range(count):
+        direct(source, 0).wait()
+        for kind in range(1, peers):
+            direct(source, kind).wait_send()
+            forward(source, kind).wait()
+
+
 def gather_features(attended):
     count = lax.axis_size("req")
     heads = lax.axis_size("head")
-    quarter = lax.all_to_all(attended, "head", 0, 1, tiled=True)
-    part = lax.all_to_all(quarter, "req", 1, 0, tiled=True)
-    full = lax.all_gather(part, "head", axis=0, tiled=False)
-    rows = attended.shape[0] // heads
-    full = full.reshape(heads, count, rows, part.shape[1])
-    return jnp.transpose(full, (1, 0, 2, 3)).reshape(count * attended.shape[0], part.shape[1])
+    width = attended.shape[1] * heads // count
+    sems = pltpu.SemaphoreType.DMA
+    return pl.pallas_call(
+        functools.partial(gather_kernel, count, heads),
+        out_shape=jax.ShapeDtypeStruct((count * attended.shape[0], width), attended.dtype),
+        in_specs=[pl.BlockSpec(memory_space=pl.ANY)],
+        out_specs=pl.BlockSpec(memory_space=pl.ANY),
+        scratch_shapes=[
+            sems((count,)),
+            sems((count,)),
+            sems,
+            sems((heads // 2, count)),
+            sems((heads // 2, count)),
+            sems((heads // 2, count)),
+            sems((heads // 2, count)),
+        ],
+        compiler_params=pltpu.CompilerParams(collective_id=0, has_side_effects=True),
+    )(attended)
+
+
+def sum_kernel(count, heads, x_ref, out_ref, from_heads, part, from_reqs, whole, sh, rh, sr, rr, sg, rg, sw, rw):
+    r = lax.axis_index("req")
+    h = lax.axis_index("head")
+    big = part.shape[0]
+    small = big // count
+    barrier = pltpu.get_barrier_semaphore()
+    for step in range(1, heads):
+        greet(barrier, req=r, head=(h + step) % heads)
+    for step in range(1, count):
+        greet(barrier, req=(r + step) % count, head=h)
+    pl.semaphore_wait(barrier, heads + count - 2)
+
+    def cut(index, size):
+        return pl.ds(pl.multiple_of(index * size, size), size)
+
+    copies = []
+    for step in range(1, heads):
+        peer = (h + step) % heads
+        copies.append(
+            remote(x_ref.at[cut(peer, big)], from_heads.at[step], sh.at[step], rh.at[step], req=r, head=peer)
+        )
+        copies[-1].start()
+    total = x_ref[cut(h, big)]
+    for step, copy in enumerate(copies):
+        copy.wait()
+        total = total + from_heads[step + 1]
+    part[...] = total
+    copies = []
+    for step in range(1, count):
+        peer = (r + step) % count
+        copies.append(
+            remote(part.at[cut(peer, small)], from_reqs.at[step], sr.at[step], rr.at[step], req=peer, head=h)
+        )
+        copies[-1].start()
+    total = part[cut(r, small)]
+    for step, copy in enumerate(copies):
+        copy.wait()
+        total = total + from_reqs[step + 1]
+    mine = pl.ds(pl.multiple_of(h * big + r * small, small), small)
+    whole[mine] = total
+    copies = []
+    for step in range(1, count):
+        peer = (r + step) % count
+        copies.append(
+            remote(whole.at[mine], whole.at[mine], sg.at[step], rg.at[step], req=peer, head=h)
+        )
+        copies[-1].start()
+    for copy in copies:
+        copy.wait()
+    copies = []
+    for step in range(1, heads):
+        peer = (h + step) % heads
+        spot = whole.at[cut(h, big)]
+        copies.append(remote(spot, spot, sw.at[step], rw.at[step], req=r, head=peer))
+        copies[-1].start()
+    for copy in copies:
+        copy.wait()
+    out_ref[...] = whole[...]
+
+
+def sum_everywhere(part):
+    count = lax.axis_size("req")
+    heads = lax.axis_size("head")
+    groups = 128 // part.shape[1]
+    size = part.shape[0] // groups
+    packed = jnp.concatenate([part[k * size : (k + 1) * size] for k in range(groups)], axis=1)
+    big = size // heads
+    sems = pltpu.SemaphoreType.DMA
+    total = pl.pallas_call(
+        functools.partial(sum_kernel, count, heads),
+        out_shape=jax.ShapeDtypeStruct(packed.shape, packed.dtype),
+        in_specs=[pl.BlockSpec(memory_space=pltpu.VMEM)],
+        out_specs=pl.BlockSpec(memory_space=pltpu.VMEM),
+        scratch_shapes=[
+            pltpu.VMEM((heads, big, 128), jnp.float32),
+            pltpu.VMEM((big, 128), jnp.float32),
+            pltpu.VMEM((count, big // count, 128), jnp.float32),
+            pltpu.VMEM((size, 128), jnp.float32),
+            sems((heads,)),
+            sems((heads,)),
+            sems((count,)),
+            sems((count,)),
+            sems((count,)),
+            sems((count,)),
+            sems((heads,)),
+            sems((heads,)),
+        ],
+        compiler_params=pltpu.CompilerParams(collective_id=1, has_side_effects=True),
+    )(packed)
+    width = part.shape[1]
+    return jnp.concatenate(
+        [total[:, k * width : (k + 1) * width] for k in range(groups)], axis=0
+    )
+
+
+def scatter_kernel(outer, chunks, a_ref, w_ref, s_ref, u_ref, out_ref, given, taken, kept, up, down,
+                   send_p, recv_p, send_l, recv_u, recv_d):
+    rows, cols = out_ref.shape
+    width = cols // chunks
+    r = lax.axis_index("req")
+    a, b = r // 2, r % 2
+    barrier = pltpu.get_barrier_semaphore()
+    greet(barrier, req=2 * a + 1 - b)
+
+    @pl.when(a > 0)
+    def _():
+        greet(barrier, req=r - 2)
+
+    @pl.when(a < outer - 1)
+    def _():
+        greet(barrier, req=r + 2)
+
+    inside = jnp.logical_and(a > 0, a < outer - 1)
+
+    @pl.when(inside)
+    def _():
+        pl.semaphore_wait(barrier, 3)
+
+    @pl.when(jnp.logical_not(inside))
+    def _():
+        pl.semaphore_wait(barrier, 2)
+
+    def goal(step):
+        result = a
+        for place in range(outer):
+            order = sorted(range(outer), key=lambda t: (-abs(t - place), t))
+            for at in range(outer):
+                result = jnp.where(jnp.logical_and(a == place, step == at), order[at], result)
+        return result
+
+    def product(target, inner, chunk):
+        block = pl.ds(pl.multiple_of((target * 2 + inner) * rows, rows), rows)
+        span = pl.ds(pl.multiple_of(chunk * width, width), width)
+        value = jnp.dot(a_ref[block, :], w_ref[:, span], preferred_element_type=jnp.float32)
+        return value + jnp.dot(s_ref[block, :], u_ref[:, span], preferred_element_type=jnp.float32)
+
+    def pair(target, chunk):
+        return remote(
+            given.at[target, chunk], taken.at[target, chunk], send_p.at[target, chunk],
+            recv_p.at[target, chunk], req=2 * a + 1 - b,
+        )
+
+    def higher(target, chunk):
+        return remote(
+            kept.at[target, chunk], up.at[target, chunk], send_l.at[target, chunk],
+            recv_u.at[target, chunk], req=r + 2,
+        )
+
+    def lower(target, chunk):
+        return remote(
+            kept.at[target, chunk], down.at[target, chunk], send_l.at[target, chunk],
+            recv_d.at[target, chunk], req=r - 2,
+        )
+
+    def give(unit, carry):
+        target, chunk = goal(unit // chunks), unit % chunks
+        given[target, chunk] = product(target, 1 - b, chunk).astype(given.dtype)
+        pair(target, chunk).start()
+        return carry
+
+    lax.fori_loop(0, outer * chunks, give, 0)
+
+    def reduce(unit, carry):
+        target, chunk = goal(unit // chunks), unit % chunks
+        value = product(target, b, chunk)
+        pair(target, chunk).wait_recv()
+        value = value + taken[target, chunk].astype(jnp.float32)
+
+        @pl.when(jnp.logical_and(target > a, a == 0))
+        def _():
+            kept[target, chunk] = value.astype(kept.dtype)
+
+        @pl.when(jnp.logical_and(target > a, a > 0))
+        def _():
+            higher(target, chunk).wait_recv()
+            kept[target, chunk] = (value + up[target, chunk].astype(jnp.float32)).astype(kept.dtype)
+
+        @pl.when(target > a)
+        def _():
+            higher(target, chunk).start()
+
+        @pl.when(jnp.logical_and(target < a, a == outer - 1))
+        def _():
+            kept[target, chunk] = value.astype(kept.dtype)
+
+        @pl.when(jnp.logical_and(target < a, a < outer - 1))
+        def _():
+            lower(target, chunk).wait_recv()
+            kept[target, chunk] = (value + down[target, chunk].astype(jnp.float32)).astype(kept.dtype)
+
+        @pl.when(target < a)
+        def _():
+            lower(target, chunk).start()
+
+        span = pl.ds(pl.multiple_of(chunk * width, width), width)
+
+        @pl.when(jnp.logical_and(target == a, a == 0))
+        def _():
+            lower(target, chunk).wait_recv()
+            out_ref[:, span] = (value + down[target, chunk].astype(jnp.float32)).astype(out_ref.dtype)
+
+        @pl.when(jnp.logical_and(target == a, a == outer - 1))
+        def _():
+            higher(target, chunk).wait_recv()
+            out_ref[:, span] = (value + up[target, chunk].astype(jnp.float32)).astype(out_ref.dtype)
+
+        @pl.when(jnp.logical_and(target == a, jnp.logical_and(a > 0, a < outer - 1)))
+        def _():
+            higher(target, chunk).wait_recv()
+            lower(target, chunk).wait_recv()
+            both = up[target, chunk].astype(jnp.float32) + down[target, chunk].astype(jnp.float32)
+            out_ref[:, span] = (value + both).astype(out_ref.dtype)
+
+        return carry
+
+    lax.fori_loop(0, outer * chunks, reduce, 0)
+
+    def finish(unit, carry):
+        target, chunk = unit // chunks, unit % chunks
+        pair(target, chunk).wait_send()
+        pl.when(target > a)(higher(target, chunk).wait_send)
+        pl.when(target < a)(lower(target, chunk).wait_send)
+        return carry
+
+    lax.fori_loop(0, outer * chunks, finish, 0)
+
+
+def scatter_products(block, weights, spread, lifts):
+    count = lax.axis_size("req")
+    outer = count // 2
+    chunks = 4
+    rows = block.shape[0] // count
+    cols = weights.shape[1]
+    slots = pltpu.VMEM((outer, chunks, rows, cols // chunks), jnp.bfloat16)
+    sems = pltpu.SemaphoreType.DMA((outer, chunks))
+    return pl.pallas_call(
+        functools.partial(scatter_kernel, outer, chunks),
+        out_shape=jax.ShapeDtypeStruct((rows, cols), jnp.bfloat16),
+        in_specs=[pl.BlockSpec(memory_space=pltpu.VMEM)] * 4,
+        out_specs=pl.BlockSpec(memory_space=pltpu.VMEM),
+        scratch_shapes=[slots] * 5 + [sems] * 5,
+        compiler_params=pltpu.CompilerParams(
+            collective_id=2, has_side_effects=True, vmem_limit_bytes=52 * 1024 * 1024
+        ),
+    )(block, weights, spread, lifts)
 
 
 def shrink(block, tenants, weights, first):
@@ -132,13 +499,9 @@
     down_count = down.shape[1] // RANK
     up_count = adapter_up.shape[0] // RANK
     part = shrink(block, tenants, down, lax.axis_index("head") * down_count)
-    shrunk = lax.psum(part, ("req", "head")).astype(jnp.bfloat16)
+    shrunk = sum_everywhere(part).astype(jnp.bfloat16)
     spread = spread_tenants(shrunk, tenants, up_count, lax.axis_index("req") * up_count)
-    mixed = jnp.dot(block, out_weight, preferred_element_type=jnp.float32)
-    mixed = mixed + jnp.dot(spread, adapter_up, preferred_element_type=jnp.float32)
-    return lax.psum_scatter(
-        mixed.astype(jnp.bfloat16), "req", scatter_dimension=0, tiled=True
-    )
+    return scatter_products(block, out_weight, spread, adapter_up)
 
 
 def solution(mesh):

time: 445 us -> 322 us (0.72)
  Pallas kernels: 0 us -> 246 us
  blocking collectives: 184 us -> 16.5 us
  waiting for transfers between devices: 149 us -> 0.01 us
  matrix products: 37.8 us -> 12.2 us
  local copies, waits for them, and re-layouts: 39.4 us -> 25.7 us
  between operations: 14.5 us -> 1.01 us
    pallas_call x0 -> x3, Pallas kernels: none -> 246 us  [the longest x1 126 us: gather_features(): pl.pallas_call(functools.partial(gather_kernel, count, heads), out_shape=...]
    reduce_scatter x1 -> x0, waiting for transfers between devices: 149 us -> none  [local(): lax.psum_scatter(mixed.astype(jnp.bfloat16), 'req', scatter_dimension=0,...]
    psum x1 -> x0, blocking collectives: 85.1 us -> none  [local(): shrunk = lax.psum(part, ('req', 'head')).astype(jnp.bfloat16)]
    all_to_all x2 -> x0, blocking collectives: 50.6 us -> none  [the longest x1 31.9 us: gather_features(): part = lax.all_to_all(quarter, 'req', 1, 0, tiled=True)]
    all_gather x1, blocking collectives: 48.2 us -> 16.5 us  [local(): tenants = lax.all_gather(tenant_ids, 'req', axis=0, tiled=True)]
    dot_general x2 -> x0, matrix products: 25.5 us -> none  [the longest x1 15.2 us: local(): mixed = jnp.dot(block, out_weight, preferred_element_type=jnp.float32)]
  transfers between devices with their start and end apart: 4 -> 2, of which waited for: 1 -> 0; matrix products, arithmetic and copies ran while one was open for 4% -> 6% of each run, Pallas kernels for 0% -> 39%
where the time goes in v2:
time: 322 us; the launch traced here: 321 us
  Pallas kernels  246 us (76%)
  local copies, waits for them, and re-layouts  25.7 us (8%)
  blocking collectives  16.5 us (5%)
  starting transfers between devices  12.4 us (4%)
  matrix products  12.2 us (4%)
  other arithmetic  7.77 us (2%)
    pallas_call x1, Pallas kernels, gather_features(): pl.pallas_call(functools.partial(gather_kernel, count, heads), out_shape=...  126 us
    pallas_call x1, Pallas kernels, scatter_products(): pl.pallas_call(functools.partial(scatter_kernel, outer, chunks), out_shap...  99.3 us
    pallas_call x1, Pallas kernels, sum_everywhere(): pl.pallas_call(functools.partial(sum_kernel, count, heads), out_shape=jax...  20.3 us
    all_gather x1, blocking collectives, local(): tenants = lax.all_gather(tenant_ids, 'req', axis=0, tiled=True)  16.5 us
    ppermute x2, starting transfers between devices, reshard_down(): received.append(lax.ppermute(piece, ('req', 'head'), pairs))  12.4 us
    dot_general x1, matrix products, shrink(): product = jnp.dot(block, weights, preferred_element_type=jnp.float32)  7.42 us
  transfers between devices with their start and end apart: 2, of which 0 were waited for; matrix products, arithmetic and copies ran while one was open for 6% of the time, Pallas kernels for 39%

profile of v2, /device:TPU:0, one launch (start us, length us, event | category | flops | bytes accessed | tf_op | source)
XLA Modules:
  0.0 321.1 jit_solution(1256325352068052333)
XLA Ops:
  0.0 0.0 copy-start
  0.0 0.0 copy-start.5
  0.0 0.0 copy-start.4
  0.0 3.2 dynamic-slice_bitcast_fusion.1
  3.2 3.0 collective-permute-start.1
  6.1 9.4 %collective-permute-start = (bf16[1024,512]{1,0:T(8,128)(2,1)}, bf16[1024,512]{1,0:T(8,128)(2,1)}, u32[]{:S(2)}, u32[]{:S(2)}) collective-permute-start(bf16[1024,512]{1,0:T(8,128)(2,1)} %get-tuple-element.8), channel_id=1, source_target_pairs={{0,0},{1,8},{2,16},{3,24},{4,4},{5,12},{6,20},{7,28},{8,1},{9,9},{... | collective-permute-start | bytes 3145736 | tf_op jit(solution)/shard_map/ppermute | solution.py:41
  16.3 0.0 copy-done.5
  16.3 1.9 constant_dynamic-slice_fusion
  18.2 0.2 copy.74
  18.4 0.3 copy.46
  18.7 0.0 copy-done.4
  18.7 0.2 copy.48
  18.9 0.3 copy.49
  19.2 0.8 gather_fusion.2
  20.0 1.7 gather_fusion.3
  21.6 1.2 copy.73
  22.9 0.3 copy.44
  23.2 1.7 gather_fusion.1
  24.8 1.2 copy.53
  26.1 0.3 copy.54
  26.3 1.7 gather_fusion.4
  28.1 0.0 copy-start.3
  28.1 0.0 copy-done
  28.1 0.8 bitcast_reduce_fusion
  28.8 0.5 copy-done.3
  29.3 0.9 fusion.3
  30.2 0.0 copy-start.1
  30.2 1.7 fusion.7
  32.0 0.0 copy-done.1
  32.0 0.0 copy-start.2
  32.0 1.4 fusion.8
  33.4 0.0 copy-done.2
  33.4 1.6 add_convert_fusion
  35.1 0.0 copy-start.6
  35.1 1.4 copy.72.x_ref
  36.5 125.8 %shard_map.100.a_ref = bf16[2048,1024]{1,0:T(8,128)(2,1)} custom-call(bf16[256,2048]{1,0:T(8,128)(2,1)} %copy.72.x_ref), custom_call_target="tpu_custom_call" | custom-call | tf_op jit(solution)/shard_map/pallas_call | solution.py:157
  162.4 0.0 copy-done.6
  162.4 16.5 %all-gather = s32[8,1,256]{2,1,0:T(1,128)S(1)} all-gather(s32[1,1,256]{2,1,0:T(1,128)S(1)} %bitcast.101), channel_id=1, replica_groups=mesh['req'=8,'head'=4] {'req'}, dimensions={0}, use_global_device_ids=true | all-gather | bytes 9216 | tf_op jit(solution)/shard_map/all_gather | solution.py:496
  178.9 0.1 broadcast_compare_fusion.1
  179.0 0.1 broadcast_compare_fusion
  179.1 0.0 collective-permute-done.1
  179.1 0.0 collective-permute-done
  179.1 1.7 pad_maximum_fusion
  180.9 2.0 gather_fusion
  182.9 1.9 select_bitcast_fusion
  184.7 2.5 copy.58
  187.3 7.4 %select_reduce_fusion = f32[2048,32]{0,1:T(8,128)S(1)} fusion(pred[2048,32]{0,1:T(8,128)(4,1)S(1)} %broadcast_compare_fusion, bf16[32,32,1024]{2,1,0:T(8,128)(2,1)} %bitcast.93, bf16[2048,1024]{1,0:T(8,128)(2,1)} %shard_map.100.a_ref), kind=kOutput, calls=%fused_computation.5 | convolution fusion | flops 4299096064 | bytes 6619136 | tf_op jit(solution)/shard_map/dot_general | solution.py:424
  194.7 0.1 copy.78
  194.8 0.1 copy.77
  195.0 0.1 copy.76
  195.1 0.1 copy.75
  195.2 1.0 pad_maximum_fusion.1.x_ref
  196.2 20.3 %shard_map.101 = f32[512,128]{1,0:T(8,128)} custom-call(f32[512,128]{1,0:T(8,128)} %pad_maximum_fusion.1.x_ref), custom_call_target="tpu_custom_call" | custom-call | tf_op jit(solution)/shard_map/pallas_call | solution.py:243
  216.6 1.0 convert.10
  217.5 0.2 fusion.45
  217.7 0.1 copy.66
  217.8 0.1 copy.65
  217.9 0.1 copy.64
  218.0 0.1 copy.63
  218.1 0.2 broadcast_select_fusion
  218.3 2.5 copy.67.s_ref
  220.8 99.3 %shard_map.102 = bf16[256,2048]{1,0:T(8,128)(2,1)S(1)} custom-call(bf16[2048,1024]{1,0:T(8,128)(2,1)} %shard_map.100.a_ref, bf16[1024,2048]{1,0:T(8,128)(2,1)} %w_ref.1, bf16[2048,512]{1,0:T(8,128)(2,1)} %copy.67.s_ref, bf16[512,2048]{1,0:T(8,128)(2,1)} %u_ref.1), custom_call_target="tpu_custom_call" | custom-call | tf_op jit(solution)/shard_map/pallas_call | solution.py:410
  320.2 1.0 copy.94
  (13 shorter events, 0.1 us)
Async XLA Ops:
  0.0 28.1 %copy-start = (bf16[256,2048]{1,0:T(8,128)(2,1)S(1)}, bf16[256,2048]{1,0:T(8,128)(2,1)}, u32[]{:S(2)}) copy-start(bf16[256,2048]{1,0:T(8,128)(2,1)} %param.12) | copy-start | bytes 3145732
  0.0 16.3 %copy-start.5 = (bf16[2,256,1024]{2,1,0:T(8,128)(2,1)S(1)}, bf16[2,256,1024]{2,1,0:T(8,128)(2,1)}, u32[]{:S(2)}) copy-start(bf16[2,256,1024]{2,1,0:T(8,128)(2,1)} %param.15) | copy-start | bytes 3145732
  0.0 18.7 %copy-start.4 = (bf16[256,1024]{1,0:T(8,128)(2,1)S(1)}, bf16[256,1024]{1,0:T(8,128)(2,1)}, u32[]{:S(2)}) copy-start(bf16[256,1024]{1,0:T(8,128)(2,1)} %param.13) | copy-start | bytes 1572868
  3.2 176.0 %collective-permute-start.1 = (bf16[1024,512]{1,0:T(8,128)(2,1)}, bf16[1024,512]{1,0:T(8,128)(2,1)}, u32[]{:S(2)}, u32[]{:S(2)}) collective-permute-start(bf16[1024,512]{1,0:T(8,128)(2,1)} %get-tuple-element.9), channel_id=1, source_target_pairs={{0,4},{1,12},{2,20},{3,28},{4,0},{5,8},{6,16},{7,24},{8,5},{9,13},... | collective-permute-start | bytes 3145736 | tf_op jit(solution)/shard_map/ppermute | solution.py:41
  6.1 173.0 %collective-permute-start = (bf16[1024,512]{1,0:T(8,128)(2,1)}, bf16[1024,512]{1,0:T(8,128)(2,1)}, u32[]{:S(2)}, u32[]{:S(2)}) collective-permute-start(bf16[1024,512]{1,0:T(8,128)(2,1)} %get-tuple-element.8), channel_id=1, source_target_pairs={{0,0},{1,8},{2,16},{3,24},{4,4},{5,12},{6,20},{7,28},{8,1},{9,9},{... | collective-permute-start | bytes 3145736 | tf_op jit(solution)/shard_map/ppermute | solution.py:41
  28.1 1.2 copy-start.3
  30.2 1.7 copy-start.1
  32.0 1.5 copy-start.2
  35.1 127.3 %copy-start.6 = (s32[256]{0:T(256)S(1)}, s32[256]{0:T(256)}, u32[]{:S(2)}) copy-start(s32[256]{0:T(256)} %param.18) | copy-start | bytes 3076

commit v3 on v2

--- a/solution.py
+++ b/solution.py
@@ -60,7 +60,7 @@
     pl.semaphore_signal(barrier, inc=1, device_id=axis, device_id_type=pl.DeviceIdType.MESH)
 
 
-def gather_kernel(count, heads, x_ref, out_ref, send_a, recv_a, local_sem, send_b, recv_b, send_c, recv_c):
+def gather_kernel(count, heads, x_ref, ids_ref, out_ref, all_ref, send_t, recv_t, send_a, recv_a, local_sem, send_b, recv_b, send_c, recv_c):
     fold = count // heads
     rows = x_ref.shape[0]
     share = rows // heads
@@ -78,13 +78,16 @@
     for step in range(1, heads):
         greet(barrier, req=r, head=(h + step) % heads)
 
+    for step in range(1, count):
+        greet(barrier, req=(r + step) % count, head=h)
+
     @pl.when(h == owner)
     def _():
-        pl.semaphore_wait(barrier, count + heads - 2)
+        pl.semaphore_wait(barrier, 2 * count + heads - 3)
 
     @pl.when(h != owner)
     def _():
-        pl.semaphore_wait(barrier, count + heads - 1)
+        pl.semaphore_wait(barrier, 2 * count + heads - 2)
 
     def place(source, quarter):
         return out_ref.at[pl.ds(pl.multiple_of(source * rows + quarter * share, share), share), :]
@@ -107,6 +110,16 @@
         pl.when(far)(copy.start)
         pl.when(jnp.logical_not(far))(near.start)
 
+    ids = []
+    for step in range(1, count):
+        ids.append(
+            remote(
+                ids_ref, all_ref.at[r], send_t.at[step], recv_t.at[step], req=(r + step) % count, head=h
+            )
+        )
+        ids[-1].start()
+    all_ref[r] = ids_ref[...]
+
     def direct(source, kind):
         head = twin if kind == 0 else (h + 2 * kind) % heads
         spot = place(source, h)
@@ -139,6 +152,8 @@
         if step:
             pass_on((source + 1) % count)
     pass_on((r + 1) % count)
+    for copy in ids:
+        copy.wait()
     for step in range(count):
         far, copy, near = first(step)
         pl.when(far)(copy.wait_send)
@@ -149,17 +164,23 @@
             forward(source, kind).wait()
 
 
-def gather_features(attended):
+def gather_features(attended, tenant_ids):
     count = lax.axis_size("req")
     heads = lax.axis_size("head")
     width = attended.shape[1] * heads // count
     sems = pltpu.SemaphoreType.DMA
-    return pl.pallas_call(
+    ids = tenant_ids.reshape(-1, 128)
+    block, tenants = pl.pallas_call(
         functools.partial(gather_kernel, count, heads),
-        out_shape=jax.ShapeDtypeStruct((count * attended.shape[0], width), attended.dtype),
-        in_specs=[pl.BlockSpec(memory_space=pl.ANY)],
-        out_specs=pl.BlockSpec(memory_space=pl.ANY),
+        out_shape=(
+            jax.ShapeDtypeStruct((count * attended.shape[0], width), attended.dtype),
+            jax.ShapeDtypeStruct((count, *ids.shape), ids.dtype),
+        ),
+        in_specs=[pl.BlockSpec(memory_space=pltpu.VMEM)] * 2,
+        out_specs=(pl.BlockSpec(memory_space=pltpu.VMEM),) * 2,
         scratch_shapes=[
+            sems((count,)),
+            sems((count,)),
             sems((count,)),
             sems((count,)),
             sems,
@@ -168,8 +189,11 @@
             sems((heads // 2, count)),
             sems((heads // 2, count)),
         ],
-        compiler_params=pltpu.CompilerParams(collective_id=0, has_side_effects=True),
-    )(attended)
+        compiler_params=pltpu.CompilerParams(
+            collective_id=0, has_side_effects=True, vmem_limit_bytes=32 * 1024 * 1024
+        ),
+    )(attended, ids)
+    return block, tenants.reshape(-1)
 
 
 def sum_kernel(count, heads, x_ref, out_ref, from_heads, part, from_reqs, whole, sh, rh, sr, rr, sg, rg, sw, rw):
@@ -493,9 +517,8 @@
     adapter_up,
 ):
     down = reshard_down(adapter_down)
-    tenants = lax.all_gather(tenant_ids, "req", axis=0, tiled=True)
     attended = attention(queries, new_keys, new_values, cache_keys, cache_values, request_slot)
-    block = gather_features(attended)
+    block, tenants = gather_features(attended, tenant_ids)
     down_count = down.shape[1] // RANK
     up_count = adapter_up.shape[0] // RANK
     part = shrink(block, tenants, down, lax.axis_index("head") * down_count)

time: 322 us -> 310 us (0.963)
  blocking collectives: 16.5 us -> 0 us
    all_gather x1 -> x0, blocking collectives: 16.5 us -> none  [local(): tenants = lax.all_gather(tenant_ids, 'req', axis=0, tiled=True)]
    unnamed x23 -> x25, local copies, waits for them, and re-layouts: 4.84 us -> 6.78 us
  transfers between devices with their start and end apart: 2 -> 2, of which waited for: 0 -> 0; matrix products, arithmetic and copies ran while one was open for 6% -> 6% of each run, Pallas kernels for 39% -> 41%
where the time goes in v3:
time: 310 us; the launch traced here: 309 us
  Pallas kernels  248 us (80%)
  local copies, waits for them, and re-layouts  26.9 us (9%)
  starting transfers between devices  12.4 us (4%)
  matrix products  12.2 us (4%)
  other arithmetic  7.84 us (3%)
    pallas_call x1, Pallas kernels, gather_features(): pl.pallas_call(functools.partial(gather_kernel, count, heads), out_shape=...  125 us
    pallas_call x1, Pallas kernels, scatter_products(): pl.pallas_call(functools.partial(scatter_kernel, outer, chunks), out_shap...  99.5 us
    pallas_call x1, Pallas kernels, sum_everywhere(): pl.pallas_call(functools.partial(sum_kernel, count, heads), out_shape=jax...  23.3 us
    ppermute x2, starting transfers between devices, reshard_down(): received.append(lax.ppermute(piece, ('req', 'head'), pairs))  12.4 us
    dot_general x1, matrix products, shrink(): product = jnp.dot(block, weights, preferred_element_type=jnp.float32)  7.43 us
    unnamed x25, local copies, waits for them, and re-layouts  6.78 us
  transfers between devices with their start and end apart: 2, of which 0 were waited for; matrix products, arithmetic and copies ran while one was open for 6% of the time, Pallas kernels for 41%

profile of v3, /device:TPU:0, one launch (start us, length us, event | category | flops | bytes accessed | tf_op | source)
XLA Modules:
  0.0 308.6 jit_solution(17221502657516057929)
XLA Ops:
  0.0 0.0 copy-start
  0.0 0.0 copy-start.7
  0.0 0.0 copy-start.6
  0.0 3.1 %dynamic-slice_bitcast_fusion.1 = (bf16[1024,512]{1,0:T(8,128)(2,1)}, bf16[1024,512]{1,0:T(8,128)(2,1)}) fusion(bf16[2,1024,512]{2,1,0:T(8,128)(2,1)} %bitcast.95, s32[]{:T(128)S(6)} %select_n.106, s32[]{:T(128)S(6)} %select_n.108), kind=kLoop, calls=%fused_computation.38 | loop fusion | bytes 4194312 | tf_op jit(solution)/shard_map/jit(dynamic_index_in_dim)/squeeze | solution.py:34
  3.1 3.0 collective-permute-start.1
  6.1 9.4 %collective-permute-start = (bf16[1024,512]{1,0:T(8,128)(2,1)}, bf16[1024,512]{1,0:T(8,128)(2,1)}, u32[]{:S(2)}, u32[]{:S(2)}) collective-permute-start(bf16[1024,512]{1,0:T(8,128)(2,1)} %get-tuple-element.12), channel_id=1, source_target_pairs={{0,0},{1,8},{2,16},{3,24},{4,4},{5,12},{6,20},{7,28},{8,1},{9,9},{... | collective-permute-start | bytes 3145736 | tf_op jit(solution)/shard_map/ppermute | solution.py:41
  16.3 0.0 copy-done.7
  16.3 1.9 constant_dynamic-slice_fusion
  18.2 0.2 copy.74
  18.4 0.3 copy.46
  18.7 0.0 copy-done.6
  18.7 0.2 copy.48
  19.0 0.3 copy.49
  19.2 0.8 gather_fusion.2
  20.0 1.7 gather_fusion.3
  21.6 1.2 copy.73
  22.9 0.3 copy.44
  23.2 1.7 gather_fusion.1
  24.8 1.2 copy.53
  26.1 0.3 copy.54
  26.3 1.7 gather_fusion.4
  28.0 0.0 copy-start.5
  28.0 0.0 copy-done
  28.0 0.8 bitcast_reduce_fusion
  28.8 0.4 copy-done.5
  29.3 0.9 fusion.3
  30.2 0.0 copy-start.3
  30.2 1.8 fusion.7
  32.0 0.0 copy-done.3
  32.0 0.0 copy-start.4
  32.1 1.4 fusion.8
  33.5 0.0 copy-done.4
  33.5 0.0 copy-start.2
  33.5 1.6 add_convert_fusion
  35.2 0.6 copy.72.x_ref
  35.8 0.0 copy-done.2
  35.8 125.4 %shard_map.100 = (bf16[2048,1024]{1,0:T(8,128)(2,1)S(1)}, s32[8,2,128]{2,1,0:T(2,128)S(1)}) custom-call(bf16[256,2048]{1,0:T(8,128)(2,1)S(1)} %copy.72.x_ref, s32[2,128]{1,0:T(2,128)S(1)} %bitcast.93), custom_call_target="tpu_custom_call" | custom-call | tf_op jit(solution)/shard_map/pallas_call | solution.py:173
  161.3 0.0 copy-start.1
  161.3 1.9 copy-done.1
  163.2 0.1 broadcast_compare_fusion.1
  163.3 0.1 broadcast_compare_fusion
  163.4 0.0 collective-permute-done.1
  163.4 0.0 collective-permute-done
  163.5 1.7 pad_maximum_fusion
  165.2 2.0 gather_fusion
  167.2 1.9 select_bitcast_fusion
  169.0 2.6 copy.58
  171.6 7.4 %select_reduce_fusion = f32[2048,32]{0,1:T(8,128)S(1)} fusion(pred[2048,32]{0,1:T(8,128)(4,1)S(1)} %broadcast_compare_fusion, bf16[32,32,1024]{2,1,0:T(8,128)(2,1)} %bitcast.96, bf16[2048,1024]{1,0:T(8,128)(2,1)} %copy-done.1), kind=kOutput, calls=%fused_computation.5 | convolution fusion | flops 4299096064 | bytes 6619136 | tf_op jit(solution)/shard_map/dot_general | solution.py:448
  179.1 0.1 copy.78
  179.2 0.1 copy.77
  179.3 0.1 copy.76
  179.5 0.1 copy.75
  179.6 1.0 pad_maximum_fusion.1.x_ref
  180.6 23.3 %shard_map.101 = f32[512,128]{1,0:T(8,128)} custom-call(f32[512,128]{1,0:T(8,128)} %pad_maximum_fusion.1.x_ref), custom_call_target="tpu_custom_call" | custom-call | tf_op jit(solution)/shard_map/pallas_call | solution.py:267
  203.9 1.0 convert.10
  204.9 0.2 fusion.45
  205.1 0.1 copy.66
  205.2 0.1 copy.65
  205.2 0.1 copy.64
  205.3 0.1 copy.63
  205.5 0.2 broadcast_select_fusion
  205.7 2.5 copy.67.s_ref
  208.2 99.5 %shard_map.102 = bf16[256,2048]{1,0:T(8,128)(2,1)S(1)} custom-call(bf16[2048,1024]{1,0:T(8,128)(2,1)} %copy-done.1, bf16[1024,2048]{1,0:T(8,128)(2,1)} %w_ref.1, bf16[2048,512]{1,0:T(8,128)(2,1)} %copy.67.s_ref, bf16[512,2048]{1,0:T(8,128)(2,1)} %u_ref.1), custom_call_target="tpu_custom_call" | custom-call | tf_op jit(solution)/shard_map/pallas_call | solution.py:434
  307.7 1.0 copy.94
  (13 shorter events, 0.1 us)
Async XLA Ops:
  0.0 28.0 %copy-start = (bf16[256,2048]{1,0:T(8,128)(2,1)S(1)}, bf16[256,2048]{1,0:T(8,128)(2,1)}, u32[]{:S(2)}) copy-start(bf16[256,2048]{1,0:T(8,128)(2,1)} %param.12) | copy-start | bytes 3145732
  0.0 16.3 %copy-start.7 = (bf16[2,256,1024]{2,1,0:T(8,128)(2,1)S(1)}, bf16[2,256,1024]{2,1,0:T(8,128)(2,1)}, u32[]{:S(2)}) copy-start(bf16[2,256,1024]{2,1,0:T(8,128)(2,1)} %param.15) | copy-start | bytes 3145732
  0.0 18.7 %copy-start.6 = (bf16[256,1024]{1,0:T(8,128)(2,1)S(1)}, bf16[256,1024]{1,0:T(8,128)(2,1)}, u32[]{:S(2)}) copy-start(bf16[256,1024]{1,0:T(8,128)(2,1)} %param.13) | copy-start | bytes 1572868
  3.1 160.3 %collective-permute-start.1 = (bf16[1024,512]{1,0:T(8,128)(2,1)}, bf16[1024,512]{1,0:T(8,128)(2,1)}, u32[]{:S(2)}, u32[]{:S(2)}) collective-permute-start(bf16[1024,512]{1,0:T(8,128)(2,1)} %get-tuple-element.13), channel_id=1, source_target_pairs={{0,4},{1,12},{2,20},{3,28},{4,0},{5,8},{6,16},{7,24},{8,5},{9,13},... | collective-permute-start | bytes 3145736 | tf_op jit(solution)/shard_map/ppermute | solution.py:41
  6.1 157.3 %collective-permute-start = (bf16[1024,512]{1,0:T(8,128)(2,1)}, bf16[1024,512]{1,0:T(8,128)(2,1)}, u32[]{:S(2)}, u32[]{:S(2)}) collective-permute-start(bf16[1024,512]{1,0:T(8,128)(2,1)} %get-tuple-element.12), channel_id=1, source_target_pairs={{0,0},{1,8},{2,16},{3,24},{4,4},{5,12},{6,20},{7,28},{8,1},{9,9},{... | collective-permute-start | bytes 3145736 | tf_op jit(solution)/shard_map/ppermute | solution.py:41
  28.0 1.2 copy-start.5
  30.2 1.8 copy-start.3
  32.0 1.4 copy-start.4
  33.5 2.3 copy-start.2
  161.3 1.9 copy-start.1
